TPU v7x, 512 devices: a whole 4x4x16 slice. The times are simulated.
512 devices in a mesh: row: 32 (over x, y, core), col: 16 (over z).
Axes of the slice: x: 4, y: 4, z: 16, core: 2. Of those that a mesh axis runs over, the one named last changes fastest.
Arguments:
- diag_factor: float32 [1024, 1024], P('row', 'col'), may hold values from -1 to 2.5, as said below
- panel_factor: float32 [16384, 1024], P('row', 'col'), may hold values from -0.046875 to 0.046875
- left_factor: float32 [16384, 8192], P('row', 'col'), may hold values from -0.046875 to 0.046875
- pivot_factor: float32 [1024, 8192], P('row', 'col'), may hold values from -0.1875 to 0.1875
- panel_adjoint: float32 [16384, 1024], P('row', 'col'), may hold values from -6 to 6
- left_adjoint: float32 [16384, 8192], P('row', 'col'), may hold values from -6 to 6
- pivot_adjoint: float32 [1024, 8192], P('row', 'col'), may hold values from -6 to 6
- diag_adjoint: float32 [1024, 1024], P('row', 'col'), may hold values from -6 to 6
Outputs:
- solved_panel: float32 [16384, 1024], P('row', 'col')
- left_out: float32 [16384, 8192], P('row', 'col')
- pivot_out: float32 [1024, 8192], P('row', 'col')
- diag_out: float32 [1024, 1024], P('row', 'col')
Inputs may be any that keep to these rules, and one draw needn't show every extreme that they name: diag_factor is lower triangular: zero above the diagonal, diagonal entries at least 1.
All inputs are finite; a program needn't handle non-finite values.
Results may differ from a plain program's by a relative error of at most 0.000073.
Values sent between devices are 32-bit elements; how exact they have to be, the bound alone decides.
A program may use at most 64 MiB of HBM per device.

v0:
```python
import jax
import jax.numpy as jnp
from jax import lax
from jax.sharding import PartitionSpec as P


def right_solve(tile, source):
    return jax.scipy.linalg.solve_triangular(tile, source.T, trans="T", lower=True).T


def local(
    diag_factor,
    panel_factor,
    left_factor,
    pivot_factor,
    panel_adjoint,
    left_adjoint,
    pivot_adjoint,
    diag_adjoint,
):
    highest = lax.Precision.HIGHEST
    block_width = panel_adjoint.shape[1]
    my_col = lax.axis_index("col")
    my_row = lax.axis_index("row")
    column_block = lax.all_gather(diag_factor, "row", axis=0, tiled=True)
    whole_diag = lax.all_gather(column_block, "col", axis=1, tiled=True)
    full_rows = lax.all_gather(panel_adjoint, "col", axis=1, tiled=True)
    solved = right_solve(whole_diag, full_rows)
    solved_panel = lax.dynamic_slice_in_dim(solved, my_col * block_width, block_width, 1)
    picked = solved
    left_out = left_adjoint - jnp.dot(
        picked,
        lax.all_gather(pivot_factor, "row", axis=0, tiled=True),
        precision=highest,
        preferred_element_type=jnp.float32,
    )
    own_rows = diag_adjoint.shape[0]
    picked = solved
    pivot_sum = lax.psum_scatter(
        jnp.einsum("rk,rc->kc", picked, left_factor, precision=highest),
        "row",
        scatter_dimension=0,
        tiled=True,
    )
    picked = solved
    square_sum = lax.psum_scatter(
        jnp.einsum("rk,rc->kc", picked, panel_factor, precision=highest),
        "row",
        scatter_dimension=0,
        tiled=True,
    )
    pivot_out = pivot_adjoint - pivot_sum
    global_row = my_row * own_rows + lax.broadcasted_iota(jnp.int32, (own_rows, block_width), 0)
    global_col = my_col * block_width + lax.broadcasted_iota(jnp.int32, (own_rows, block_width), 1)
    diag_out = diag_adjoint - jnp.where(global_col <= global_row, square_sum, 0.0)
    return (solved_panel, left_out, pivot_out, diag_out)


def solution(mesh):
    in_specs = (
        P("row", "col"),
        P("row", "col"),
        P("row", "col"),
        P("row", "col"),
        P("row", "col"),
        P("row", "col"),
        P("row", "col"),
        P("row", "col"),
    )
    out_specs = (P("row", "col"), P("row", "col"), P("row", "col"), P("row", "col"))
    return jax.shard_map(local, mesh=mesh, in_specs=in_specs, out_specs=out_specs, check_vma=False)
```

profile of v0, /device:TPU:2, one launch (start us, length us, event | category | flops | bytes accessed | tf_op | source)
XLA Modules:
  0.0 463.6 jit_solution(8965409141635587499)
XLA Ops:
  7.2 27.8 %all_gather.12 = f32[1024,64]{1,0:T(8,128)S(1)} all-gather(f32[32,64]{1,0:T(8,128)} %param.8), channel_id=1, replica_groups=mesh['row'=32,'col'=16] {'row'}, dimensions={0}, use_global_device_ids=true | all-gather | bytes 270336 | tf_op jit(solution)/shard_map/all_gather | solution.py:25
  35.0 0.9 copy.14
  36.0 0.7 all-gather.6.cloned.1.call-update
  36.7 0.7 all-gather.8.cloned.1.call-update
  37.5 77.2 %all-gather.4.cloned.1.call-done = f32[1024,1024]{0,1:T(8,128)} async-done(((f32[1024,64]{0,1:T(8,128)}), f32[1024,1024]{0,1:T(8,128)}) %all-gather.4.cloned.1.call-update) | async-done | bytes 4194320 | tf_op jit(solution)/shard_map/all_gather | solution.py:26
  114.7 4.8 %fusion = f32[1024,1024]{0,1:T(8,128)} fusion(f32[1024,1024]{0,1:T(8,128)} %all-gather.4.cloned.1.call-done), kind=kLoop, calls=%fused_computation.3 | loop fusion | flops 2097152 | bytes 8388608 | tf_op jit(solution)/shard_map/jit(_solve_triangular)/triangular_solve | solution.py:8
  119.5 24.1 %while.1 = (s32[]{:T(128)}, f32[1024,1024]{0,1:T(8,128)}, s32[8,2]{0,1:T(2,128)S(1)}, f32[8,128,128]{2,1,0:T(8,128)S(1)}, s32[]{:T(128)}) while((s32[]{:T(128)}, f32[1024,1024]{0,1:T(8,128)}, s32[8,2]{0,1:T(2,128)S(1)}, f32[8,128,128]{2,1,0:T(8,128)S(1)}, s32[]{:T(128)}) %tuple.28), condition=%wide.while_cond, body=%wide.while_body.sunk | while | flops 2 | bytes 393321 | solution.py:8
  120.1 2.3 dynamic-slice.12
  123.1 2.3 dynamic-slice.12
  126.1 2.3 dynamic-slice.12
  129.1 2.3 dynamic-slice.12
  132.2 2.3 dynamic-slice.12
  135.2 2.3 dynamic-slice.12
  138.2 2.3 dynamic-slice.12
  141.2 2.2 dynamic-slice.12
  143.6 78.6 %custom-call.4 = f32[8,128,128]{1,2,0:T(8,128)S(1)} custom-call(f32[8,128,128]{2,1,0:T(8,128)S(1)} %get-tuple-element.11), custom_call_target="InvertDiagBlocksLowerTriangular" | custom-call | tf_op jit(solution)/shard_map/jit(_solve_triangular)/triangular_solve | solution.py:8
  222.2 1.5 fusion.19
  223.8 1.4 convolution_subtract_fusion.4
  225.5 1.4 convolution_subtract_fusion.3
  227.3 1.6 convolution_subtract_fusion.6
  229.3 1.7 convolution_subtract_fusion.7
  231.4 1.9 convolution_subtract_fusion.2
  233.8 2.0 convolution_subtract_fusion.5
  236.4 2.2 convolution_subtract_fusion.1
  238.6 1.2 convolution_dynamic-update-slice_fusion
  240.1 2.6 fusion.36
  243.0 4.8 %fusion.35 = f32[1024,512]{1,0:T(8,128)} fusion(f32[1024,512]{1,0:T(8,128)S(1)} %constant_dynamic-update-slice_fusion.18, f32[512,512]{1,0:T(8,128)S(1)} %copy-done), kind=kOutput, calls=%fused_computation.85 | convolution fusion | flops 3221225472 | bytes 5242880 | tf_op jit(solution)/shard_map/rk,rc->kc/dot_general | solution.py:40
  248.5 6.3 %convolution_subtract_fusion = f32[512,512]{1,0:T(8,128)} fusion(f32[512,512]{1,0:T(8,128)} %param.13, f32[1024,512]{1,0:T(8,128)S(1)} %constant_dynamic-update-slice_fusion.18, f32[1024,512]{1,0:T(8,128)} %all-gather.8.cloned.1.call-done), kind=kOutput, calls=%fused_computation.4 | convolution fusion | flops 3221487616 | bytes 6291456 | tf_op jit(solution)/shard_map/dot_general | solution.py:31
  254.9 95.1 %reduce-scatter.5.cloned.1.call-done = f32[32,64]{1,0:T(8,128)} async-done(((f32[1024,64]{1,0:T(8,128)}), f32[32,64]{1,0:T(8,128)}) %reduce-scatter.5.cloned.1.call-update) | async-done | bytes 8208 | tf_op jit(solution)/shard_map/reduce_scatter | solution.py:46
  349.9 1.4 select_subtract_fusion
  351.3 104.3 %reduce-scatter.3.cloned.1.call-done = f32[32,512]{1,0:T(8,128)} async-done(((f32[1024,512]{1,0:T(8,128)}), f32[32,512]{1,0:T(8,128)}) %reduce-scatter.3.cloned.1.call-update) | async-done | bytes 65552 | tf_op jit(solution)/shard_map/reduce_scatter | solution.py:39
  455.6 1.5 sub.10
  (88 shorter events, 9.4 us)
Async XLA Ops:
  7.2 235.8 %copy-start = (f32[512,512]{1,0:T(8,128)S(1)}, f32[512,512]{1,0:T(8,128)}, u32[]{:S(2)}) copy-start(f32[512,512]{1,0:T(8,128)} %param.10) | copy-start | bytes 3145732
  7.2 107.5 %all-gather.4.cloned.1.call-start = ((), (), s32[]{:S(2)}) async-start(), calls=%async_computation.2 | async-start | bytes 4456448 | tf_op jit(solution)/shard_map/all_gather | solution.py:26
  35.9 186.3 %all-gather.6.cloned.1.call-start = ((), (), s32[]{:S(2)}) async-start(), calls=%async_computation.3 | async-start | bytes 2228224 | tf_op jit(solution)/shard_map/all_gather | solution.py:27
  36.7 211.8 %all-gather.8.cloned.1.call-start = ((), (), s32[]{:S(2)}) async-start(), calls=%async_computation.4 | async-start | bytes 2162688 | tf_op jit(solution)/shard_map/all_gather | solution.py:33
  37.4 312.5 %reduce-scatter.5.cloned.1.call-start = ((), (), s32[]{:S(2)}) async-start(), calls=%async_computation.6 | async-start | bytes 540672 | tf_op jit(solution)/shard_map/reduce_scatter | solution.py:46
  222.2 13.7 %copy-start.2 = (f32[8,128,128]{1,2,0:T(8,128)}, f32[8,128,128]{1,2,0:T(8,128)S(1)}, u32[]{:S(2)}) copy-start(f32[8,128,128]{1,2,0:T(8,128)S(1)} %custom-call.4) | copy-start | bytes 1572868
  222.2 5.1 %copy-start.1 = (f32[512,1024]{0,1:T(8,128)S(1)}, f32[512,1024]{0,1:T(8,128)}, u32[]{:S(2)}) copy-start(f32[512,1024]{0,1:T(8,128)} %all-gather.6.cloned.1.call-done) | copy-start | bytes 6291460
  238.6 1.5 copy-start.3
  242.7 212.9 %reduce-scatter.3.cloned.1.call-start = ((), (), s32[]{:S(2)}) async-start(), calls=%async_computation.5 | async-start | bytes 2162688 | tf_op jit(solution)/shard_map/reduce_scatter | solution.py:39
  248.5 101.4 %copy-start.5 = (f32[32,64]{1,0:T(8,128)S(1)}, f32[32,64]{1,0:T(8,128)}, u32[]{:S(2)}) copy-start(f32[32,64]{1,0:T(8,128)} %param.15) | copy-start | bytes 24580
  248.5 207.1 %copy-start.4 = (f32[32,512]{1,0:T(8,128)S(1)}, f32[32,512]{1,0:T(8,128)}, u32[]{:S(2)}) copy-start(f32[32,512]{1,0:T(8,128)} %param.14) | copy-start | bytes 196612
Sparse Core Ops, SparseCore 0:
  36.0 78.6 all-gather.3
  116.8 70.5 all-gather.5
  190.5 55.6 all-gather.7
  250.3 99.5 reduce-scatter.4
  354.2 101.3 reduce-scatter.2
where the time goes:
time: 465 us; the launch traced here: 464 us
  waiting for transfers between devices  278 us (60%)
  other arithmetic  86.2 us (19%)
  matrix products  30.8 us (7%)
  blocking collectives  27.8 us (6%)
  local copies, waits for them, and re-layouts  25.9 us (6%)
  between operations  14.2 us (3%)
    reduce_scatter x1, waiting for transfers between devices, local(): lax.psum_scatter(jnp.einsum('rk,rc->kc', picked, left_factor, precision=h...  104 us
    reduce_scatter x1, waiting for transfers between devices, local(): lax.psum_scatter(jnp.einsum('rk,rc->kc', picked, panel_factor, precision=...  95.1 us
    another operation x3, other arithmetic, right_solve(): jax.scipy.linalg.solve_triangular(tile, source.T, trans='T', lower=True)  83.4 us
    all_gather x1, waiting for transfers between devices, local(): whole_diag = lax.all_gather(column_block, 'col', axis=1, tiled=True)  77.2 us
    all_gather x1, blocking collectives, local(): column_block = lax.all_gather(diag_factor, 'row', axis=0, tiled=True)  27.8 us
    another operation x40, local copies, waits for them, and re-layouts  23.8 us
    another operation x15, matrix products, right_solve(): jax.scipy.linalg.solve_triangular(tile, source.T, trans='T', lower=True)  17.1 us
  transfers between devices with their start and end apart: 5, of which 3 were waited for; matrix products, arithmetic and copies ran while one was open for 30% of the time, Pallas kernels for 0%

commit v1 on v0

--- a/solution.py
+++ b/solution.py
@@ -23,7 +23,9 @@
     my_col = lax.axis_index("col")
     my_row = lax.axis_index("row")
     column_block = lax.all_gather(diag_factor, "row", axis=0, tiled=True)
-    whole_diag = lax.all_gather(column_block, "col", axis=1, tiled=True)
+    whole_diag = jnp.concatenate(
+        lax.all_to_all(jnp.stack([column_block] * lax.axis_size("col")), "col", 0, 0), axis=1
+    )
     full_rows = lax.all_gather(panel_adjoint, "col", axis=1, tiled=True)
     solved = right_solve(whole_diag, full_rows)
     solved_panel = lax.dynamic_slice_in_dim(solved, my_col * block_width, block_width, 1)

time: 465 us -> 594 us (1.28)
  waiting for transfers between devices: 278 us -> 394 us
  starting transfers between devices: 0.42 us -> 12.8 us
    all_to_all x0 -> x1, waiting for transfers between devices: none -> 202 us  [local(): lax.all_to_all(jnp.stack([column_block] * lax.axis_size('col')), 'col', 0...]
    all_gather x1 -> x0, waiting for transfers between devices: 77.2 us -> none  [local(): whole_diag = lax.all_gather(column_block, 'col', axis=1, tiled=True)]
    all_to_all x0 -> x1, starting transfers between devices: none -> 12.4 us  [local(): lax.all_to_all(jnp.stack([column_block] * lax.axis_size('col')), 'col', 0...]
    reduce_scatter x1, waiting for transfers between devices: 95.1 us -> 85.7 us  [local(): lax.psum_scatter(jnp.einsum('rk,rc->kc', picked, panel_factor, precision=...]
    another operation x40 -> x41, local copies, waits for them, and re-layouts: 23.8 us -> 26.4 us
  transfers between devices with their start and end apart: 5 -> 5, of which waited for: 3 -> 3; matrix products, arithmetic and copies ran while one was open for 30% -> 24% of each run, Pallas kernels for 0% -> 0%
where the time goes in v1:
time: 594 us
  waiting for transfers between devices  394 us (66%)
  other arithmetic  86.3 us (15%)
  matrix products  30.8 us (5%)
  blocking collectives  27.8 us (5%)
  local copies, waits for them, and re-layouts  27.7 us (5%)
  between operations  14.2 us (2%)
  starting transfers between devices  12.8 us (2%)
    all_to_all x1, waiting for transfers between devices, local(): lax.all_to_all(jnp.stack([column_block] * lax.axis_size('col')), 'col', 0...  202 us
    reduce_scatter x1, waiting for transfers between devices, local(): lax.psum_scatter(jnp.einsum('rk,rc->kc', picked, left_factor, precision=h...  104 us
    reduce_scatter x1, waiting for transfers between devices, local(): lax.psum_scatter(jnp.einsum('rk,rc->kc', picked, panel_factor, precision=...  85.7 us
    another operation x3, other arithmetic, right_solve(): jax.scipy.linalg.solve_triangular(tile, source.T, trans='T', lower=True)  83.4 us
    all_gather x1, blocking collectives, local(): column_block = lax.all_gather(diag_factor, 'row', axis=0, tiled=True)  27.8 us
    another operation x40, local copies, waits for them, and re-layouts  23.9 us
    another operation x15, matrix products, right_solve(): jax.scipy.linalg.solve_triangular(tile, source.T, trans='T', lower=True)  17.1 us
    all_to_all x1, starting transfers between devices, local(): lax.all_to_all(jnp.stack([column_block] * lax.axis_size('col')), 'col', 0...  12.4 us
  transfers between devices with their start and end apart: 5, of which 3 were waited for; matrix products, arithmetic and copies ran while one was open for 24% of the time, Pallas kernels for 0%

profile of v1, /device:TPU:2, one launch (start us, length us, event | category | flops | bytes accessed | tf_op | source)
XLA Modules:
  0.0 593.5 jit_solution(3380108188413443091)
XLA Ops:
  7.2 27.8 %all_gather.9 = f32[1024,64]{1,0:T(8,128)S(1)} all-gather(f32[32,64]{1,0:T(8,128)} %param.8), channel_id=1, replica_groups=mesh['row'=32,'col'=16] {'row'}, dimensions={0}, use_global_device_ids=true | all-gather | bytes 270336 | tf_op jit(solution)/shard_map/all_gather | solution.py:25
  35.1 2.5 stack.2
  37.7 12.4 %all-to-all-start = ((f32[16,1024,64]{1,2,0:T(8,128)}), f32[16,1024,64]{1,2,0:T(8,128)}, u32[]{:S(2)}, u32[]{:S(2)}) async-start(f32[16,1024,64]{1,2,0:T(8,128)} %stack.2), calls=%async_computation | async-start | bytes 8388608 | tf_op jit(solution)/shard_map/all_to_all | solution.py:27
  50.8 0.7 all-gather.5.cloned.1.call-update
  51.6 202.3 %all-to-all-done = f32[16,1024,64]{1,2,0:T(8,128)} async-done(((f32[16,1024,64]{1,2,0:T(8,128)}), f32[16,1024,64]{1,2,0:T(8,128)}, u32[]{:S(2)}, u32[]{:S(2)}) %all-to-all-start) | async-done | bytes 4194336 | tf_op jit(solution)/shard_map/all_to_all | solution.py:27
  253.9 4.8 bitcast_select_fusion
  258.7 24.1 %while.1 = (s32[]{:T(128)}, f32[1024,1024]{0,1:T(8,128)}, s32[8,2]{0,1:T(2,128)S(1)}, f32[8,128,128]{2,1,0:T(8,128)S(1)}, s32[]{:T(128)}) while((s32[]{:T(128)}, f32[1024,1024]{0,1:T(8,128)}, s32[8,2]{0,1:T(2,128)S(1)}, f32[8,128,128]{2,1,0:T(8,128)S(1)}, s32[]{:T(128)}) %tuple.27), condition=%wide.while_cond, body=%wide.while_body.sunk | while | flops 2 | bytes 393321 | solution.py:8
  259.3 2.3 dynamic-slice.12
  262.3 2.3 dynamic-slice.12
  265.3 2.3 dynamic-slice.12
  268.4 2.3 dynamic-slice.12
  271.4 2.3 dynamic-slice.12
  274.4 2.3 dynamic-slice.12
  277.4 2.3 dynamic-slice.12
  280.5 2.2 dynamic-slice.12
  282.8 78.6 %custom-call.4 = f32[8,128,128]{1,2,0:T(8,128)S(1)} custom-call(f32[8,128,128]{2,1,0:T(8,128)S(1)} %get-tuple-element.11), custom_call_target="InvertDiagBlocksLowerTriangular" | custom-call | tf_op jit(solution)/shard_map/jit(_solve_triangular)/triangular_solve | solution.py:8
  361.5 1.5 fusion.18
  363.0 1.4 convolution_subtract_fusion.4
  364.7 1.4 convolution_subtract_fusion.3
  366.6 1.6 convolution_subtract_fusion.6
  368.5 1.7 convolution_subtract_fusion.7
  370.7 1.9 convolution_subtract_fusion.2
  373.1 2.0 convolution_subtract_fusion.5
  375.6 2.2 convolution_subtract_fusion.1
  377.9 1.2 convolution_dynamic-update-slice_fusion
  379.3 2.6 fusion.35
  382.2 4.8 fusion.34
  387.8 6.4 %convolution_subtract_fusion = f32[512,512]{1,0:T(8,128)} fusion(f32[512,512]{1,0:T(8,128)} %param.13, f32[1024,512]{1,0:T(8,128)S(1)} %constant_dynamic-update-slice_fusion.18, f32[1024,512]{1,0:T(8,128)} %all-gather.5.cloned.1.call-done), kind=kOutput, calls=%fused_computation.4 | convolution fusion | flops 3221487616 | bytes 6291456 | tf_op jit(solution)/shard_map/dot_general | solution.py:33
  394.1 85.7 %reduce-scatter.5.cloned.1.call-done = f32[32,64]{1,0:T(8,128)} async-done(((f32[1024,64]{1,0:T(8,128)}), f32[32,64]{1,0:T(8,128)}) %reduce-scatter.5.cloned.1.call-update) | async-done | bytes 8208 | tf_op jit(solution)/shard_map/reduce_scatter | solution.py:48
  479.8 1.4 select_subtract_fusion
  481.2 104.3 %reduce-scatter.3.cloned.1.call-done = f32[32,512]{1,0:T(8,128)} async-done(((f32[1024,512]{1,0:T(8,128)}), f32[32,512]{1,0:T(8,128)}) %reduce-scatter.3.cloned.1.call-update) | async-done | bytes 65552 | tf_op jit(solution)/shard_map/reduce_scatter | solution.py:41
  585.5 1.5 sub.10
  (88 shorter events, 10.2 us)
Async XLA Ops:
  7.2 375.1 %copy-start = (f32[512,512]{1,0:T(8,128)S(1)}, f32[512,512]{1,0:T(8,128)}, u32[]{:S(2)}) copy-start(f32[512,512]{1,0:T(8,128)} %param.10) | copy-start | bytes 3145732
  37.7 216.3 %all-to-all-start = ((f32[16,1024,64]{1,2,0:T(8,128)}), f32[16,1024,64]{1,2,0:T(8,128)}, u32[]{:S(2)}, u32[]{:S(2)}) async-start(f32[16,1024,64]{1,2,0:T(8,128)} %stack.2), calls=%async_computation | async-start | bytes 8388608 | tf_op jit(solution)/shard_map/all_to_all | solution.py:27
  50.1 311.4 %all-gather.3.cloned.1.call-start = ((), (), s32[]{:S(2)}) async-start(), calls=%async_computation.3 | async-start | bytes 2228224 | tf_op jit(solution)/shard_map/all_gather | solution.py:29
  50.8 337.0 %all-gather.5.cloned.1.call-start = ((), (), s32[]{:S(2)}) async-start(), calls=%async_computation.4 | async-start | bytes 2162688 | tf_op jit(solution)/shard_map/all_gather | solution.py:35
  51.5 428.3 %reduce-scatter.5.cloned.1.call-start = ((), (), s32[]{:S(2)}) async-start(), calls=%async_computation.6 | async-start | bytes 540672 | tf_op jit(solution)/shard_map/reduce_scatter | solution.py:48
  361.4 13.7 %copy-start.2 = (f32[8,128,128]{1,2,0:T(8,128)}, f32[8,128,128]{1,2,0:T(8,128)S(1)}, u32[]{:S(2)}) copy-start(f32[8,128,128]{1,2,0:T(8,128)S(1)} %custom-call.4) | copy-start | bytes 1572868
  361.5 5.1 copy-start.1
  377.9 1.5 copy-start.3
  381.9 203.6 %reduce-scatter.3.cloned.1.call-start = ((), (), s32[]{:S(2)}) async-start(), calls=%async_computation.5 | async-start | bytes 2162688 | tf_op jit(solution)/shard_map/reduce_scatter | solution.py:41
  387.7 92.1 %copy-start.5 = (f32[32,64]{1,0:T(8,128)S(1)}, f32[32,64]{1,0:T(8,128)}, u32[]{:S(2)}) copy-start(f32[32,64]{1,0:T(8,128)} %param.15) | copy-start | bytes 24580
  387.7 197.8 %copy-start.4 = (f32[32,512]{1,0:T(8,128)S(1)}, f32[32,512]{1,0:T(8,128)}, u32[]{:S(2)}) copy-start(f32[32,512]{1,0:T(8,128)} %param.14) | copy-start | bytes 196612
Sparse Core Ops, SparseCore 0:
  53.0 177.8 all-gather.2
  234.0 76.9 all-gather.4
  382.1 97.7 reduce-scatter.4
  484.1 101.3 reduce-scatter.2
